TPU v7x, 128 devices: a whole 4x4x4 slice. The times are simulated.
128 devices in a mesh: row: 8 (over x, core), col: 16 (over z, y).
Axes of the slice: x: 4, y: 4, z: 4, core: 2. Of those that a mesh axis runs over, the one named last changes fastest.
Arguments:
- sources: bfloat16 [64, 262144], P(None, 'row'), may hold values from -2 to 2
- targets: bfloat16 [64, 262144], P(None, 'col'), may hold values from -2 to 3, as said below
- log_a: float32 [262144], P('row'), may hold values from -6 to 0
- log_b: float32 [262144], P('col'), may hold values from -6 to 0
- block_cols: int32 [1024, 32], P('row', 'col'), may hold values from 0 to 63, as said below
- block_count: int32 [1024, 16], P('row', 'col'), may hold values from 0 to 2, as said below
Outputs:
- f_potential: float32 [262144], P('row')
- g_potential: float32 [262144], P('col')
Inputs may be any that keep to these rules, and one draw needn't show every extreme that they name: `targets`: targets are real points; coordinates stay in the stated range. `block_cols`: slot numbers index column blocks of their own column shard; the used slots of one row block and shard name distinct blocks; slots at or beyond the count hold 0 and are ignored. Every column block is named by some row block. `block_count`: every row block uses at least one slot over all column shards.
All inputs are finite; a program needn't handle non-finite values.
Results may differ from a plain program's by a relative error of at most 0.0003.
Values sent between devices are 32-bit elements; how exact they have to be, the bound alone decides.
A program may use at most 64 MiB of HBM per device.

v0:
```python
import functools

import jax
import jax.numpy as jnp
from jax import lax
from jax.experimental import pallas as pl
from jax.experimental.pallas import tpu as pltpu
from jax.sharding import PartitionSpec as P

BLOCK = 256
ITERS = 2
EPS = 0.05
LOG2_SCALE = 20.0 * 1.4426950408889634
NEG = -1e30
UNROLL = 4
AUG = 16
THRESHOLD = 2.0**-90
MESH = pl.DeviceIdType.MESH


def build_pairs(cols_ref, count_ref, pair_a, pair_b, npairs, row_blocks, slots):
    def add(b, n):
        used = count_ref[b]
        for s in range(slots):
            pair_a[n] = b
            pair_b[n] = cols_ref[b * slots + s]
            n = n + (s < used).astype(jnp.int32)
        return n

    total = lax.fori_loop(0, row_blocks, add, jnp.int32(0), unroll=4)
    for k in range(UNROLL):
        pair_a[total + k] = jnp.int32(-1)
        pair_b[total + k] = jnp.int32(-1)
    npairs[0] = total


def split3(v):
    hi = v.astype(jnp.bfloat16).astype(jnp.float32)
    rest = v - hi
    mid = rest.astype(jnp.bfloat16).astype(jnp.float32)
    return hi, mid, rest - mid


def half_norms(points_ref, out_ref, blocks):
    def one(b, carry):
        blk = points_ref[:, pl.ds(pl.multiple_of(b * BLOCK, BLOCK), BLOCK)].astype(jnp.float32)
        out_ref[pl.ds(b, 1), :] = 0.5 * jnp.sum(blk * blk, 0, keepdims=True)
        return carry

    lax.fori_loop(0, blocks, one, 0, unroll=4)


def pass_body(
    bias, red_ref, keep_ref, pot_red, pot_keep, pair_red, pair_keep, npairs_ref,
    rel_ref, red_parts, keep_parts, acc, top, touched,
):
    nred = pot_red.shape[0]
    nkeep = pot_keep.shape[0]
    npairs = npairs_ref[0]
    for part, value in enumerate(split3(pot_red[...])):
        red_parts[part] = value
    for part, value in enumerate(split3(pot_keep[...] + bias / LOG2_SCALE)):
        keep_parts[part] = value
    acc[...] = jnp.zeros_like(acc)
    touched[...] = jnp.zeros_like(touched)
    line = lax.broadcasted_iota(jnp.int32, (8, BLOCK), 0)
    zeros = jnp.zeros((8, BLOCK), jnp.float32)

    def rows(parts, index, first, ones):
        out = jnp.where((line >= ones) & (line < ones + 3), 1.0, 0.0)
        for part in range(3):
            out = jnp.where(line == first + part, parts[part, pl.ds(index, 1), :], out)
        return jnp.concatenate([out, zeros], 0).astype(jnp.bfloat16)

    def scores(p):
        slot_r = pair_red[p]
        slot_k = pair_keep[p]
        r = jnp.maximum(slot_r, 0)
        k = jnp.maximum(slot_k, 0)
        into = jnp.where(slot_k < 0, nkeep, slot_k)
        rblk = red_ref[:, pl.ds(pl.multiple_of(r * BLOCK, BLOCK), BLOCK)]
        kblk = keep_ref[:, pl.ds(pl.multiple_of(k * BLOCK, BLOCK), BLOCK)]
        lhs = jnp.concatenate([rblk, rows(red_parts, r, 0, 3)], 0)
        rhs = jnp.concatenate([kblk, rows(keep_parts, k, 3, 0)], 0)
        z = lax.dot_general(lhs, rhs, (((0,), (0,)), ((), ())), preferred_element_type=jnp.float32)
        return z, into

    def add_pair(p, shift):
        z, into = scores(p)
        if shift is not None:
            z = z - shift[pl.ds(into, 1), :]
        e = jnp.exp2(z * LOG2_SCALE)
        acc[into] += jnp.sum(e.reshape(BLOCK // 8, 8, BLOCK), 0)
        touched[pl.ds(into, 1), :] = jnp.ones((1, BLOCK), jnp.float32)

    def group(t, carry):
        for u in range(UNROLL):
            add_pair(t * UNROLL + u, None)
        return carry

    lax.fori_loop(0, (npairs + UNROLL - 1) // UNROLL, group, 0)
    total = jnp.sum(acc[:nkeep], 1)
    live = touched[:nkeep] > 0.0
    rel_ref[...] = jnp.where(live, jnp.log2(total) - bias, NEG)
    weak = jnp.max(jnp.where(live & (total < THRESHOLD), 1.0, 0.0))

    @pl.when(weak > 0.0)
    def _():
        acc[...] = jnp.full_like(acc, NEG)

        def top_pair(p, carry):
            z, into = scores(p)
            acc[into] = jnp.maximum(acc[into], jnp.max(z.reshape(BLOCK // 8, 8, BLOCK), 0))
            return carry

        lax.fori_loop(0, npairs, top_pair, 0)
        top[:nkeep] = jnp.max(acc[:nkeep], 1)
        acc[...] = jnp.zeros_like(acc)

        def sum_pair(p, carry):
            add_pair(p, top)
            return carry

        lax.fori_loop(0, npairs, sum_pair, 0)
        fixed = jnp.log2(jnp.sum(acc[:nkeep], 1)) + (top[:nkeep] * LOG2_SCALE - bias)
        rel_ref[...] = jnp.where(touched[:nkeep] > 0.0, fixed, NEG)


def first_kernel(
    bias, slots, sources, targets, cols, counts,
    rel, half_src, half_tgt, pair_row, pair_col, npairs,
    pot_src, pot_tgt, *scratch,
):
    build_pairs(cols, counts, pair_row, pair_col, npairs, half_src.shape[0], slots)
    half_norms(sources, half_src, half_src.shape[0])
    half_norms(targets, half_tgt, half_tgt.shape[0])
    pot_src[...] = -half_src[...]
    pot_tgt[...] = -half_tgt[...]
    pass_body(bias, targets, sources, pot_tgt, pot_src, pair_col, pair_row, npairs, rel, *scratch)


VMEM = pl.BlockSpec(memory_space=pltpu.VMEM)
SMEM = pl.BlockSpec(memory_space=pltpu.SMEM)


def pass_scratch(nred, nkeep):
    return [
        pltpu.VMEM((3, nred, BLOCK), jnp.float32),
        pltpu.VMEM((3, nkeep, BLOCK), jnp.float32),
        pltpu.VMEM((nkeep + 1, 8, BLOCK), jnp.float32),
        pltpu.VMEM((nkeep + 8, BLOCK), jnp.float32),
        pltpu.VMEM((nkeep + 8, BLOCK), jnp.float32),
    ]


def local_params():
    return pltpu.CompilerParams(vmem_limit_bytes=32 * 1024 * 1024)


def first_pass(bias, slots, nred, nkeep, sources, targets, cols, counts):
    most = nkeep * slots + UNROLL
    return pl.pallas_call(
        functools.partial(first_kernel, bias, slots),
        out_shape=(
            jax.ShapeDtypeStruct((nkeep, BLOCK), jnp.float32),
            jax.ShapeDtypeStruct((nkeep, BLOCK), jnp.float32),
            jax.ShapeDtypeStruct((nred, BLOCK), jnp.float32),
            jax.ShapeDtypeStruct((most,), jnp.int32),
            jax.ShapeDtypeStruct((most,), jnp.int32),
            jax.ShapeDtypeStruct((1,), jnp.int32),
        ),
        in_specs=[VMEM, VMEM, SMEM, SMEM],
        out_specs=(VMEM, VMEM, VMEM, SMEM, SMEM, SMEM),
        scratch_shapes=[
            pltpu.VMEM((nkeep, BLOCK), jnp.float32),
            pltpu.VMEM((nred, BLOCK), jnp.float32),
        ]
        + pass_scratch(nred, nkeep),
        compiler_params=local_params(),
        name="first_pass",
    )(sources, targets, cols, counts)


def later_pass(name, bias, red, keep, pot_red, pot_keep, pair_red, pair_keep, npairs):
    nred, nkeep = pot_red.shape[0], pot_keep.shape[0]
    return pl.pallas_call(
        functools.partial(pass_body, bias),
        out_shape=jax.ShapeDtypeStruct((nkeep, BLOCK), jnp.float32),
        in_specs=[VMEM, VMEM, VMEM, VMEM, SMEM, SMEM, SMEM],
        out_specs=VMEM,
        scratch_shapes=pass_scratch(nred, nkeep),
        compiler_params=local_params(),
        name=name,
    )(red, keep, pot_red, pot_keep, pair_red, pair_keep, npairs)


def exchange_kernel(axis, n, sign, rel, old, logw, out, landing, send1, recv1, send2, recv2):
    me = lax.axis_index(axis)
    chunk = rel.shape[0] // n
    mine = pl.ds(pl.multiple_of(me * chunk, 8), chunk)

    barrier = pltpu.get_barrier_semaphore()
    for k in range(1, n):
        pl.semaphore_signal(barrier, inc=1, device_id={axis: lax.rem(me + k, n)}, device_id_type=MESH)
    pl.semaphore_wait(barrier, n - 1)

    def scatter(k):
        peer = lax.rem(me + k, n)
        return pltpu.make_async_remote_copy(
            src_ref=rel.at[pl.ds(pl.multiple_of(peer * chunk, 8), chunk)],
            dst_ref=landing.at[k - 1],
            send_sem=send1.at[k - 1],
            recv_sem=recv1.at[k - 1],
            device_id={axis: peer},
            device_id_type=MESH,
        )

    def gather(k):
        peer = lax.rem(me + k, n)
        return pltpu.make_async_remote_copy(
            src_ref=out.at[mine],
            dst_ref=out.at[mine],
            send_sem=send2.at[k - 1],
            recv_sem=recv2.at[k - 1],
            device_id={axis: peer},
            device_id_type=MESH,
        )

    first = [scatter(k) for k in range(1, n)]
    for copy in first:
        copy.start()
    own = rel[mine]
    for copy in first:
        copy.wait_recv()
    top = jnp.maximum(own, jnp.max(landing[...], 0))
    total = jnp.exp2(own - top) + jnp.sum(jnp.exp2(landing[...] - top[None]), 0)
    lse = top + jnp.log2(total)
    out[mine] = sign * old[mine] + (EPS * logw[mine] - lse * (1.0 / LOG2_SCALE))
    second = [gather(k) for k in range(1, n)]
    for copy in second:
        copy.start()
    for copy in second:
        copy.wait_recv()
    for copy in first:
        copy.wait_send()
    for copy in second:
        copy.wait_send()


def exchange(axis, n, ident, sign, rel, old, logw):
    blocks = rel.shape[0]
    return pl.pallas_call(
        functools.partial(exchange_kernel, axis, n, sign),
        out_shape=jax.ShapeDtypeStruct((blocks, BLOCK), jnp.float32),
        in_specs=[VMEM] * 3,
        out_specs=VMEM,
        scratch_shapes=[pltpu.VMEM((n - 1, blocks // n, BLOCK), jnp.float32)]
        + [pltpu.SemaphoreType.DMA((n - 1,))] * 4,
        compiler_params=pltpu.CompilerParams(collective_id=ident, has_side_effects=True),
        name=f"exchange_{axis}_{ident}",
    )(rel, old, logw)


def per_device(nrow, ncol, sources, targets, log_a, log_b, block_cols, block_count):
    row_blocks, slots = block_cols.shape
    col_blocks = targets.shape[1] // BLOCK
    log_a = log_a.reshape(row_blocks, BLOCK)
    log_b = log_b.reshape(col_blocks, BLOCK)
    row_bias, col_bias = 112.0, 104.0

    rel, half_src, half_tgt, pair_row, pair_col, npairs = first_pass(
        row_bias, slots, col_blocks, row_blocks, sources, targets, block_cols.reshape(-1), block_count.reshape(-1)
    )
    f_pot, f_sign = half_src, -1.0
    g_pot = -half_tgt
    for step in range(ITERS):
        if step > 0:
            rel = later_pass("row_pass", row_bias, targets, sources, g_pot, f_pot, pair_col, pair_row, npairs)
        f_pot = exchange("col", ncol, 2 * step, f_sign, rel, f_pot, log_a)
        f_sign = 1.0
        rel = later_pass("col_pass", col_bias, sources, targets, f_pot, g_pot, pair_row, pair_col, npairs)
        g_pot = exchange("row", nrow, 2 * step + 1, 1.0, rel, g_pot, log_b)
    return ((f_pot + half_src).reshape(-1), (g_pot + half_tgt).reshape(-1))


def solution(mesh):
    return jax.shard_map(
        functools.partial(per_device, mesh.shape["row"], mesh.shape["col"]),
        mesh=mesh,
        in_specs=(
            P(None, "row"),
            P(None, "col"),
            P("row"),
            P("col"),
            P("row", "col"),
            P("row", "col"),
        ),
        out_specs=(P("row"), P("col")),
        check_vma=False,
    )
```

profile of v0, /device:TPU:1, one launch (start us, length us, event | category | flops | bytes accessed | tf_op | source)
XLA Modules:
  0.0 228.3 jit_solution(17636460167195664801)
XLA Ops:
  0.6 1.5 reshape.25.logw
  2.1 0.8 copy.8
  2.9 0.1 reshape.22.cols
  3.0 1.6 reshape.24.logw
  4.6 0.0 copy-start
  4.6 2.2 copy-done
  6.8 0.0 copy-start.4
  6.8 1.6 copy-done.4
  8.4 0.0 copy-start.18
  8.4 0.7 copy-done.18
  9.1 0.0 copy-start.5
  9.1 29.2 %first_pass.1 = (f32[128,256]{1,0:T(8,128)S(1)}, f32[128,256]{1,0:T(8,128)S(1)}, f32[64,256]{1,0:T(8,128)S(1)}, s32[260]{0:T(512)S(1)}, s32[260]{0:T(512)S(1)}, /*index=5*/s32[1]{0:T(128)}) custom-call(bf16[64,32768]{1,0:T(8,128)(2,1)S(1)} %copy-done, bf16[64,16384]{1,0:T(8,128)(2,1)S(1)} %copy-done.4, s32[256]{0:T(256)S(1)} %reshape.22.cols, s32[128]{0:T(128)S(1)} %bitcast.7), custom_call_target="tpu_custom_call" | custom-call | tf_op jit(solution)/shard_map/first_pass/pallas_call | solution.py:162
  38.2 0.0 copy-start.12
  38.3 0.6 copy-done.12
  38.9 0.0 copy-start.17
  38.9 0.7 copy-done.17
  39.6 26.6 %exchange_col_0.1.pot_red.pot_keep.old = f32[128,256]{1,0:T(8,128)} custom-call(f32[128,256]{1,0:T(8,128)} %copy-done.17, f32[128,256]{1,0:T(8,128)} %copy-done.12, f32[128,256]{1,0:T(8,128)} %reshape.24.logw), custom_call_target="tpu_custom_call" | custom-call | tf_op jit(solution)/shard_map/exchange_col_0/pallas_call | solution.py:252
  66.1 0.0 copy-start.7
  66.2 0.0 copy-done.5
  66.2 0.0 copy-start.1
  66.2 2.2 copy-done.1
  68.4 0.0 copy-start.6
  68.4 0.9 copy-done.6
  69.3 0.0 copy-start.11
  69.3 26.0 %col_pass.2.rel = f32[64,256]{1,0:T(8,128)S(1)} custom-call(bf16[64,32768]{1,0:T(8,128)(2,1)S(1)} %copy-done.1, bf16[64,16384]{1,0:T(8,128)(2,1)S(1)} %copy-done.5, f32[128,256]{1,0:T(8,128)S(1)} %copy-done.6, f32[64,256]{1,0:T(8,128)S(1)} %neg.3.pot_keep.old, s32[260]{0:T(512)S(1)} %get-tuple-element.11.pair_red.pair_keep, ...), custom_call_target="tpu_custom_call" | custom-call | tf_op jit(solution)/shard_map/col_pass/pallas_call | solution.py:186
  95.3 0.0 copy-done.11
  95.3 0.0 copy-start.16
  95.4 0.6 copy-done.16
  96.0 0.0 copy-start.13
  96.0 37.5 %exchange_row_1.1.pot_red.pot_keep.old = f32[64,256]{1,0:T(8,128)} custom-call(f32[64,256]{1,0:T(8,128)} %copy-done.16, f32[64,256]{1,0:T(8,128)} %copy-done.11, f32[64,256]{1,0:T(8,128)} %reshape.25.logw), custom_call_target="tpu_custom_call" | custom-call | tf_op jit(solution)/shard_map/exchange_row_1/pallas_call | solution.py:252
  133.5 0.0 copy-done.7
  133.5 0.0 copy-start.2
  133.5 2.2 copy-done.2
  135.7 0.0 copy-start.9
  135.7 0.8 copy-done.9
  136.5 0.0 copy-start.10
  136.5 5.9 %row_pass.1.rel = f32[128,256]{1,0:T(8,128)S(1)} custom-call(bf16[64,16384]{1,0:T(8,128)(2,1)S(1)} %copy-done.5, bf16[64,32768]{1,0:T(8,128)(2,1)S(1)} %copy-done.2, f32[64,256]{1,0:T(8,128)S(1)} %copy-done.9, f32[128,256]{1,0:T(8,128)S(1)} %copy-done.7, s32[260]{0:T(512)S(1)} %get-tuple-element.12.pair_keep.pair_red, ...), custom_call_target="tpu_custom_call" | custom-call | tf_op jit(solution)/shard_map/row_pass/pallas_call | solution.py:186
  142.5 0.0 copy-start.14
  142.5 0.6 copy-done.14
  143.1 57.7 %exchange_col_2.1.pot_red = f32[128,256]{1,0:T(8,128)} custom-call(f32[128,256]{1,0:T(8,128)} %copy-done.14, f32[128,256]{1,0:T(8,128)} %exchange_col_0.1.pot_red.pot_keep.old, f32[128,256]{1,0:T(8,128)} %reshape.24.logw), custom_call_target="tpu_custom_call" | custom-call | tf_op jit(solution)/shard_map/exchange_col_2/pallas_call | solution.py:252
  200.9 0.0 copy-done.13
  200.9 0.9 add_bitcast_fusion
  201.8 0.0 copy-done.10
  201.8 0.0 copy-start.3
  201.8 2.2 copy-done.3
  204.0 0.0 copy-start.8
  204.0 0.9 copy-done.8
  204.9 5.6 %col_pass.3.rel = f32[64,256]{1,0:T(8,128)S(1)} custom-call(bf16[64,32768]{1,0:T(8,128)(2,1)S(1)} %copy-done.3, bf16[64,16384]{1,0:T(8,128)(2,1)S(1)} %copy-done.5, f32[128,256]{1,0:T(8,128)S(1)} %copy-done.8, f32[64,256]{1,0:T(8,128)S(1)} %copy-done.10, s32[260]{0:T(512)S(1)} %get-tuple-element.11.pair_red.pair_keep, ...), custom_call_target="tpu_custom_call" | custom-call | tf_op jit(solution)/shard_map/col_pass/pallas_call | solution.py:186
  210.5 0.0 copy-start.15
  210.5 0.6 copy-done.15
  211.1 14.9 %exchange_row_3.1 = f32[64,256]{1,0:T(8,128)} custom-call(f32[64,256]{1,0:T(8,128)} %copy-done.15, f32[64,256]{1,0:T(8,128)} %exchange_row_1.1.pot_red.pot_keep.old, f32[64,256]{1,0:T(8,128)} %reshape.25.logw), custom_call_target="tpu_custom_call" | custom-call | tf_op jit(solution)/shard_map/exchange_row_3/pallas_call | solution.py:252
  226.1 0.8 add_bitcast_fusion.1
  226.9 0.7 copy.10
  227.6 0.7 copy.9
  (1 shorter events, 0.0 us)
Async XLA Ops:
  4.6 2.2 copy-start
  6.8 1.6 copy-start.4
  8.4 0.7 copy-start.18
  9.1 57.1 %copy-start.5 = (bf16[64,16384]{1,0:T(8,128)(2,1)S(1)}, bf16[64,16384]{1,0:T(8,128)(2,1)}, u32[]{:S(2)}) copy-start(bf16[64,16384]{1,0:T(8,128)(2,1)} %keep_ref.5) | copy-start | bytes 6291460
  38.2 0.7 copy-start.12
  38.9 0.7 copy-start.17
  66.1 67.3 %copy-start.7 = (f32[128,256]{1,0:T(8,128)S(1)}, f32[128,256]{1,0:T(8,128)}, u32[]{:S(2)}) copy-start(f32[128,256]{1,0:T(8,128)} %exchange_col_0.1.pot_red.pot_keep.old) | copy-start | bytes 393220
  66.2 2.2 copy-start.1
  68.4 0.9 copy-start.6
  69.3 26.0 %copy-start.11 = (f32[64,256]{1,0:T(8,128)}, f32[64,256]{1,0:T(8,128)S(1)}, u32[]{:S(2)}) copy-start(f32[64,256]{1,0:T(8,128)S(1)} %neg.3.pot_keep.old) | copy-start | bytes 196612
  95.3 0.6 copy-start.16
  96.0 104.9 %copy-start.13 = (f32[128,256]{1,0:T(8,128)S(1)}, f32[128,256]{1,0:T(8,128)}, u32[]{:S(2)}) copy-start(f32[128,256]{1,0:T(8,128)} %copy-done.12) | copy-start | bytes 393220
  133.5 2.2 copy-start.2
  135.7 0.8 copy-start.9
  136.5 65.3 %copy-start.10 = (f32[64,256]{1,0:T(8,128)S(1)}, f32[64,256]{1,0:T(8,128)}, u32[]{:S(2)}) copy-start(f32[64,256]{1,0:T(8,128)} %exchange_row_1.1.pot_red.pot_keep.old) | copy-start | bytes 196612
  142.5 0.7 copy-start.14
  201.8 2.2 copy-start.3
  204.0 0.9 copy-start.8
  210.5 0.6 copy-start.15
where the time goes:
time: 231 us; the launch traced here: 228 us
  Pallas kernels  203 us (88%)
  local copies, waits for them, and re-layouts  22.3 us (10%)
    pallas_call x4, Pallas kernels, exchange(): pl.pallas_call(functools.partial(exchange_kernel, axis, n, sign), out_sha...  137 us
    pallas_call x3, Pallas kernels, later_pass(): pl.pallas_call(functools.partial(pass_body, bias), out_shape=jax.ShapeDty...  37.6 us
    pallas_call x1, Pallas kernels, first_pass(): pl.pallas_call(functools.partial(first_kernel, bias, slots), out_shape=(j...  29.2 us
    unnamed x41, local copies, waits for them, and re-layouts  19 us

commit v1 on v0

v1 whole, which is shorter than its diff:
```python
import functools

import jax
import jax.numpy as jnp
from jax import lax
from jax.experimental import pallas as pl
from jax.experimental.pallas import tpu as pltpu
from jax.sharding import PartitionSpec as P

BLOCK = 256
LANES = 128
ITERS = 2
EPS = 0.05
LOG2_SCALE = 20.0 * 1.4426950408889634
NEG = -1e30
BIG_GROUP = 32
SMALL_GROUP = 8
PAD = 16
CHUNKS = 4
THRESHOLD = 2.0**-90
CEILING = 2.0**120
FIRST_BIAS = 40.0
ROW_BIAS = 112.0
COL_BIAS = 104.0
MESH = pl.DeviceIdType.MESH
MIB = 1024 * 1024


def build_pairs(cols_ref, count_ref, table, row_blocks, slots):
    row_at, col_at = table_starts(table)

    def add(b, n):
        used = count_ref[0, b]
        for s in range(slots):
            table[row_at + n] = b
            table[col_at + n] = cols_ref[s, b]
            n = n + (s < used).astype(jnp.int32)
        return n

    total = lax.fori_loop(0, row_blocks, add, jnp.int32(0), unroll=8)
    for k in range(PAD):
        table[row_at + total + k] = jnp.int32(-1)
        table[col_at + total + k] = jnp.int32(-1)
    table[0] = total


def table_starts(table):
    return 8, 8 + (table.shape[0] - 8) // 2


def split3(v):
    hi = v.astype(jnp.bfloat16).astype(jnp.float32)
    rest = v - hi
    mid = rest.astype(jnp.bfloat16).astype(jnp.float32)
    return hi, mid, rest - mid


def half_norms(points, first, out_ref, start, stop):
    def one(b, carry):
        blk = points[:, pl.ds(pl.multiple_of((first + b) * BLOCK, BLOCK), BLOCK)].astype(jnp.float32)
        norm = 0.5 * jnp.sum(blk * blk, 0, keepdims=True)
        out_ref[pl.ds(2 * b, 1), :] = norm[:, :LANES]
        out_ref[pl.ds(2 * b + 1, 1), :] = norm[:, LANES:]
        return carry

    lax.fori_loop(start, stop, one, 0, unroll=4)


def lse_pass(
    bias, by_row, points, pot_red, pot_keep, table,
    rel_ref, red_parts, keep_parts, acc, top, touched,
):
    nkeep = rel_ref.shape[0] // 2
    npairs = table[0]
    keep_at, red_at = table_starts(table) if by_row else table_starts(table)[::-1]
    nred = pot_red.shape[0] // 2
    red_first, keep_first = (nkeep, 0) if by_row else (0, nred)
    shift = bias / LOG2_SCALE
    for part, value in enumerate(split3(pot_red[...])):
        red_parts[part] = value
    kept = pot_keep[...] + shift if pot_keep is not None else jnp.full(rel_ref.shape, shift, jnp.float32)
    for part, value in enumerate(split3(kept)):
        keep_parts[part] = value
    acc[...] = jnp.zeros_like(acc)
    touched[...] = jnp.zeros_like(touched)
    line = lax.broadcasted_iota(jnp.int32, (8, LANES), 0)
    zeros = jnp.zeros((8, LANES), jnp.float32)

    def rows(parts, index, first, ones):
        halves = []
        for half in range(2):
            out = jnp.where((line >= ones) & (line < ones + 3), 1.0, 0.0)
            for part in range(3):
                out = jnp.where(line == first + part, parts[part, pl.ds(2 * index + half, 1), :], out)
            halves.append(jnp.concatenate([out, zeros], 0).astype(jnp.bfloat16))
        return jnp.concatenate(halves, 1)

    def scores(p):
        slot_r = table[red_at + p]
        slot_k = table[keep_at + p]
        r = jnp.maximum(slot_r, 0)
        k = jnp.maximum(slot_k, 0)
        into = jnp.where(slot_k < 0, nkeep, slot_k)
        rblk = points[:, pl.ds(pl.multiple_of((red_first + r) * BLOCK, BLOCK), BLOCK)]
        kblk = points[:, pl.ds(pl.multiple_of((keep_first + k) * BLOCK, BLOCK), BLOCK)]
        lhs = jnp.concatenate([rblk, rows(red_parts, r, 0, 3)], 0)
        rhs = jnp.concatenate([kblk, rows(keep_parts, k, 3, 0)], 0)
        z = lax.dot_general(lhs, rhs, (((0,), (0,)), ((), ())), preferred_element_type=jnp.float32)
        return z, into

    def add_pair(p, shifted):
        z, into = scores(p)
        if shifted:
            z = z - jnp.concatenate([top[pl.ds(2 * into + half, 1), :] for half in range(2)], 1)
        part = jnp.sum(jnp.exp2(z * LOG2_SCALE), 0, keepdims=True)
        acc[pl.ds(2 * into, 1), :] += part[:, :LANES]
        acc[pl.ds(2 * into + 1, 1), :] += part[:, LANES:]
        touched[pl.ds(2 * into, 2), :] = jnp.ones((2, LANES), jnp.float32)

    def groups(size, base, trips):
        def group(t, carry):
            for u in range(size):
                add_pair(base + t * size + u, False)
            return carry

        lax.fori_loop(0, trips, group, 0)

    whole = (npairs + PAD - 1) // BIG_GROUP
    left = jnp.maximum(npairs - whole * BIG_GROUP, 0)
    groups(BIG_GROUP, 0, whole)
    groups(SMALL_GROUP, whole * BIG_GROUP, (left + SMALL_GROUP - 1) // SMALL_GROUP)
    total = acc[: 2 * nkeep]
    live = touched[: 2 * nkeep] > 0.0
    rel_ref[...] = jnp.where(live, jnp.log2(total) - bias, NEG)
    fine = (total >= THRESHOLD) & (total <= CEILING)
    weak = jnp.max(jnp.where(live & ~fine, 1.0, 0.0))

    @pl.when(weak > 0.0)
    def _():
        top[...] = jnp.full_like(top, NEG)

        def top_pair(p, carry):
            z, into = scores(p)
            part = jnp.max(z, 0, keepdims=True)
            for half in range(2):
                at = pl.ds(2 * into + half, 1)
                top[at, :] = jnp.maximum(top[at, :], part[:, half * LANES : (half + 1) * LANES])
            return carry

        lax.fori_loop(0, npairs, top_pair, 0)
        acc[...] = jnp.zeros_like(acc)

        def sum_pair(p, carry):
            add_pair(p, True)
            return carry

        lax.fori_loop(0, npairs, sum_pair, 0)
        fixed = jnp.log2(acc[: 2 * nkeep]) + (top[: 2 * nkeep] * LOG2_SCALE - bias)
        rel_ref[...] = jnp.where(touched[: 2 * nkeep] > 0.0, fixed, NEG)


def first_kernel(
    slots, sources, targets, cols, counts,
    rel, points, half_tgt, table,
    pot_tgt, cols_here, counts_here, sem_src, sem_tgt, sem_list, *scratch,
):
    row_blocks = rel.shape[0] // 2
    col_blocks = half_tgt.shape[0] // 2

    def chunk(whole, first, sem, c):
        width = whole.shape[1] // CHUNKS
        into = pl.ds(first * BLOCK + c * width, width)
        return pltpu.make_async_copy(whole.at[:, pl.ds(c * width, width)], points.at[:, into], sem.at[c])

    list_copies = [
        pltpu.make_async_copy(cols, cols_here, sem_list.at[0]),
        pltpu.make_async_copy(counts, counts_here, sem_list.at[1]),
    ]
    tgt_copies = [chunk(targets, row_blocks, sem_tgt, c) for c in range(CHUNKS)]
    src_copies = [chunk(sources, 0, sem_src, c) for c in range(CHUNKS)]
    for copy in list_copies + tgt_copies + src_copies:
        copy.start()
    for copy in list_copies:
        copy.wait()
    build_pairs(cols_here, counts_here, table, row_blocks, slots)
    for c, copy in enumerate(tgt_copies):
        copy.wait()
        half_norms(points, row_blocks, half_tgt, c * col_blocks // CHUNKS, (c + 1) * col_blocks // CHUNKS)
    pot_tgt[...] = -half_tgt[...]
    for copy in src_copies:
        copy.wait()
    lse_pass(FIRST_BIAS, True, points, pot_tgt, None, table, rel, *scratch)


def last_kernel(bias, points, f_pot, g_pot, half_src, table, rel, f_final, f_here, sem, *scratch):
    f_here[...] = f_pot[...] + half_src[...]
    copy = pltpu.make_async_copy(f_here, f_final, sem)
    copy.start()
    lse_pass(bias, False, points, f_pot, g_pot, table, rel, *scratch)
    copy.wait()


VMEM = pl.BlockSpec(memory_space=pltpu.VMEM)
SMEM = pl.BlockSpec(memory_space=pltpu.SMEM)
HBM = pl.BlockSpec(memory_space=pltpu.HBM)
ANY = pl.BlockSpec(memory_space=pl.ANY)


def pass_scratch(nred, nkeep):
    return [
        pltpu.VMEM((3, 2 * nred, LANES), jnp.float32),
        pltpu.VMEM((3, 2 * nkeep, LANES), jnp.float32),
        pltpu.VMEM((2 * nkeep + 8, LANES), jnp.float32),
        pltpu.VMEM((2 * nkeep + 8, LANES), jnp.float32),
        pltpu.VMEM((2 * nkeep + 8, LANES), jnp.float32),
    ]


def potential(blocks):
    return jax.ShapeDtypeStruct((2 * blocks, LANES), jnp.float32)


def first_pass(sources, targets, cols, counts):
    slots = cols.shape[0]
    nkeep = sources.shape[1] // BLOCK
    nred = targets.shape[1] // BLOCK
    return pl.pallas_call(
        functools.partial(first_kernel, slots),
        out_shape=(
            potential(nkeep),
            jax.ShapeDtypeStruct((sources.shape[0], sources.shape[1] + targets.shape[1]), sources.dtype),
            potential(nred),
            jax.ShapeDtypeStruct((8 + 2 * (nkeep * slots + PAD),), jnp.int32),
        ),
        in_specs=[HBM, HBM, HBM, HBM],
        out_specs=(VMEM, VMEM, VMEM, SMEM),
        scratch_shapes=[
            pltpu.VMEM((2 * nred, LANES), jnp.float32),
            pltpu.SMEM(cols.shape, jnp.int32),
            pltpu.SMEM(counts.shape, jnp.int32),
            pltpu.SemaphoreType.DMA((CHUNKS,)),
            pltpu.SemaphoreType.DMA((CHUNKS,)),
            pltpu.SemaphoreType.DMA((2,)),
        ]
        + pass_scratch(nred, nkeep),
        compiler_params=pltpu.CompilerParams(vmem_limit_bytes=24 * MIB),
        name="first_pass",
    )(*(pltpu.with_memory_space_constraint(a, pltpu.HBM) for a in (sources, targets, cols, counts)))


def later_pass(name, bias, by_row, points, pot_red, pot_keep, table, norms=None):
    nred, nkeep = pot_red.shape[0] // 2, pot_keep.shape[0] // 2
    params = pltpu.CompilerParams(vmem_limit_bytes=16 * MIB)
    if norms is None:
        return pl.pallas_call(
            functools.partial(lse_pass, bias, by_row),
            out_shape=potential(nkeep),
            in_specs=[VMEM] * 3 + [SMEM],
            out_specs=VMEM,
            scratch_shapes=pass_scratch(nred, nkeep),
            compiler_params=params,
            name=name,
        )(points, pot_red, pot_keep, table)
    return pl.pallas_call(
        functools.partial(last_kernel, bias),
        out_shape=(potential(nkeep), potential(nred)),
        in_specs=[VMEM] * 4 + [SMEM],
        out_specs=(VMEM, HBM),
        scratch_shapes=[pltpu.VMEM((2 * nred, LANES), jnp.float32), pltpu.SemaphoreType.DMA]
        + pass_scratch(nred, nkeep),
        compiler_params=params,
        name=name,
    )(points, pot_red, pot_keep, norms, table)


def offsets(outer, inner):
    def far(step):
        return min(step[0], outer - step[0]) + min(step[1], inner - step[1])

    steps = [(a, b) for a in range(outer) for b in range(inner) if a or b]
    return sorted(steps, key=lambda step: -far(step))


def exchange_kernel(axis, sides, has_old, with_norms, *refs):
    refs = list(refs)
    rel = refs.pop(0)
    old = refs.pop(0) if has_old else None
    logw = refs.pop(0)
    points = refs.pop(0) if with_norms else None
    out = refs.pop(0)
    norms = refs.pop(0) if with_norms else None
    landing, weights, wsem, send1, recv1, send2, recv2 = refs
    outer, inner = sides
    n = outer * inner
    steps = offsets(outer, inner)
    me = lax.axis_index(axis)
    peers = [
        lax.rem(me // inner + a, outer) * inner + lax.rem(lax.rem(me, inner) + b, inner) for a, b in steps
    ]
    chunk = rel.shape[0] // n
    mine = pl.ds(pl.multiple_of(me * chunk, 8), chunk)
    fetch = pltpu.make_async_copy(logw.at[mine], weights, wsem)
    fetch.start()

    barrier = pltpu.get_barrier_semaphore()
    for peer in peers:
        pl.semaphore_signal(barrier, inc=1, device_id={axis: peer}, device_id_type=MESH)
    pl.semaphore_wait(barrier, n - 1)

    def scatter(k):
        peer = peers[k]
        return pltpu.make_async_remote_copy(
            src_ref=rel.at[pl.ds(pl.multiple_of(peer * chunk, 8), chunk)],
            dst_ref=landing.at[k],
            send_sem=send1.at[k],
            recv_sem=recv1.at[k],
            device_id={axis: peer},
            device_id_type=MESH,
        )

    def gather(k):
        peer = peers[k]
        return pltpu.make_async_remote_copy(
            src_ref=out.at[mine],
            dst_ref=out.at[mine],
            send_sem=send2.at[k],
            recv_sem=recv2.at[k],
            device_id={axis: peer},
            device_id_type=MESH,
        )

    first = [scatter(k) for k in range(n - 1)]
    for copy in first:
        copy.start()
    if with_norms:
        half_norms(points, 0, norms, 0, rel.shape[0] // 2)
    own = rel[mine]
    fetch.wait()
    base = EPS * weights[...]
    if has_old:
        base = base + old[mine]
    for copy in first:
        copy.wait_recv()
    top = jnp.maximum(own, jnp.max(landing[...], 0))
    total = jnp.exp2(own - top) + jnp.sum(jnp.exp2(landing[...] - top[None]), 0)
    out[mine] = base - (top + jnp.log2(total)) * (1.0 / LOG2_SCALE)
    second = [gather(k) for k in range(n - 1)]
    for copy in second:
        copy.start()
    for copy in second:
        copy.wait_recv()
    for copy in first:
        copy.wait_send()
    for copy in second:
        copy.wait_send()


def exchange(axis, sides, ident, rel, old, logw, points=None):
    lines = rel.shape[0]
    n = sides[0] * sides[1]
    shape = jax.ShapeDtypeStruct((lines, LANES), jnp.float32)
    has_old, with_norms = old is not None, points is not None
    args = [rel] + ([old] if has_old else []) + [logw] + ([points] if with_norms else [])
    specs = [VMEM] + ([VMEM] if has_old else []) + [ANY] + ([VMEM] if with_norms else [])
    return pl.pallas_call(
        functools.partial(exchange_kernel, axis, sides, has_old, with_norms),
        out_shape=(shape, shape) if with_norms else shape,
        in_specs=specs,
        out_specs=(VMEM, VMEM) if with_norms else VMEM,
        scratch_shapes=[
            pltpu.VMEM((n - 1, lines // n, LANES), jnp.float32),
            pltpu.VMEM((lines // n, LANES), jnp.float32),
            pltpu.SemaphoreType.DMA,
        ]
        + [pltpu.SemaphoreType.DMA((n - 1,))] * 4,
        compiler_params=pltpu.CompilerParams(
            collective_id=ident, has_side_effects=True, vmem_limit_bytes=(12 if with_norms else 4) * MIB
        ),
        name=f"exchange_{axis}_{ident}",
    )(*args)


def sides_of(n):
    return (4, n // 4) if n % 4 == 0 else (n, 1)


def per_device(nrow, ncol, sources, targets, log_a, log_b, block_cols, block_count):
    row_sides, col_sides = sides_of(nrow), sides_of(ncol)
    log_a = log_a.reshape(-1, LANES)
    log_b = log_b.reshape(-1, LANES)
    rel, points, half_tgt, table = first_pass(sources, targets, block_cols.T, block_count.T)
    g_pot = -half_tgt
    f_pot = half_src = f_out = None
    for step in range(ITERS):
        if step > 0:
            rel = later_pass("row_pass", ROW_BIAS, True, points, g_pot, f_pot, table)
            f_pot = exchange("col", col_sides, 2 * step, rel, f_pot, log_a)
        else:
            f_pot, half_src = exchange("col", col_sides, 2 * step, rel, None, log_a, points)
        if step < ITERS - 1:
            rel = later_pass("col_pass", COL_BIAS, False, points, f_pot, g_pot, table)
        else:
            rel, f_out = later_pass("last_pass", COL_BIAS, False, points, f_pot, g_pot, table, half_src)
        g_pot = exchange("row", row_sides, 2 * step + 1, rel, g_pot, log_b)
    return (f_out.reshape(-1), (g_pot + half_tgt).reshape(-1))


def solution(mesh):
    return jax.shard_map(
        functools.partial(per_device, mesh.shape["row"], mesh.shape["col"]),
        mesh=mesh,
        in_specs=(
            P(None, "row"),
            P(None, "col"),
            P("row"),
            P("col"),
            P("row", "col"),
            P("row", "col"),
        ),
        out_specs=(P("row"), P("col")),
        check_vma=False,
    )
```

time: 231 us -> 157 us (0.68); the launches traced: 228 us -> 157 us
  Pallas kernels: 203 us -> 156 us
  local copies, waits for them, and re-layouts: 22.3 us -> 0.01 us
    pallas_call x8, Pallas kernels: 203 us -> 156 us  [the longest x4 84.6 us: exchange(): pl.pallas_call(functools.partial(exchange_kernel, axis, sides, has_old, w...]
    unnamed x41 -> x4, local copies, waits for them, and re-layouts: 19 us -> 0.01 us
    reshape x3 -> x0, local copies, waits for them, and re-layouts: 3.21 us -> none  [the longest x1 1.59 us: per_device(): log_a = log_a.reshape(row_blocks, BLOCK)]
where the time goes in v1:
time: 157 us
  Pallas kernels  156 us (99%)
    pallas_call x4, Pallas kernels, exchange(): pl.pallas_call(functools.partial(exchange_kernel, axis, sides, has_old, w...  84.6 us
    pallas_call x2, Pallas kernels, later_pass(): pl.pallas_call(functools.partial(lse_pass, bias, by_row), out_shape=poten...  34.2 us
    pallas_call x1, Pallas kernels, first_pass(): pl.pallas_call(functools.partial(first_kernel, slots), out_shape=(potenti...  33.5 us
    pallas_call x1, Pallas kernels, later_pass(): pl.pallas_call(functools.partial(last_kernel, bias), out_shape=(potential...  3.66 us

profile of v1, /device:TPU:1, one launch (start us, length us, event | category | flops | bytes accessed | tf_op | source)
XLA Modules:
  0.0 157.3 jit_solution(18358276915321629296)
XLA Ops:
  0.6 0.0 copy-start
  0.6 33.5 %first_pass.1 = (f32[256,128]{1,0:T(8,128)S(1)}, bf16[64,49152]{1,0:T(8,128)(2,1)S(1)}, f32[128,128]{1,0:T(8,128)S(1)}, s32[552]{0:T(1024)S(1)}) custom-call(bf16[64,32768]{1,0:T(8,128)(2,1)} %sources.1, bf16[64,16384]{1,0:T(8,128)(2,1)} %targets.1, s32[2,128]{1,0:T(2,128)} %bitcast.11, s32[1,128]{1,0:T(1,128)} %bitcast.12), custom_call_target="tpu_custom_call" | custom-call | tf_op jit(solution)/shard_map/first_pass/pallas_call | solution.py:227
  34.2 0.0 copy-done
  34.2 13.8 %exchange_col_0.1 = (f32[256,128]{1,0:T(8,128)S(1)}, f32[256,128]{1,0:T(8,128)S(1)}) custom-call(f32[256,128]{1,0:T(8,128)S(1)} %get-tuple-element.11.refs_0_, f32[256,128]{1,0:T(8,128)S(1)} %bitcast.7, bf16[64,49152]{1,0:T(8,128)(2,1)S(1)} %get-tuple-element.10.refs_2_.points), custom_call_target="tpu_custom_call" | custom-call | tf_op jit(solution)/shard_map/exchange_col_0/pallas_call | solution.py:365
  48.0 0.0 copy-start.1
  48.0 30.5 %col_pass.1.refs_0_ = f32[128,128]{1,0:T(8,128)S(1)} custom-call(bf16[64,49152]{1,0:T(8,128)(2,1)S(1)} %get-tuple-element.10.refs_2_.points, f32[256,128]{1,0:T(8,128)S(1)} %get-tuple-element.12.pot_red.pot_keep.refs_1_, f32[128,128]{1,0:T(8,128)S(1)} %neg.3.pot_keep.refs_1_, s32[552]{0:T(1024)S(1)} %get-tuple-element.14.table), custom_call_target="tpu_custom_call" | custom-call | tf_op jit(solution)/shard_map/col_pass/pallas_call | solution.py:255
  78.5 0.0 copy-done.1
  78.6 27.8 %exchange_row_1.1.pot_red.g_pot.refs_1_ = f32[128,128]{1,0:T(8,128)S(1)} custom-call(f32[128,128]{1,0:T(8,128)S(1)} %col_pass.1.refs_0_, f32[128,128]{1,0:T(8,128)S(1)} %neg.3.pot_keep.refs_1_, f32[128,128]{1,0:T(8,128)S(1)} %bitcast.9), custom_call_target="tpu_custom_call" | custom-call | tf_op jit(solution)/shard_map/exchange_row_1/pallas_call | solution.py:365
  106.4 3.7 %row_pass.1.refs_0_ = f32[256,128]{1,0:T(8,128)S(1)} custom-call(bf16[64,49152]{1,0:T(8,128)(2,1)S(1)} %get-tuple-element.10.refs_2_.points, f32[128,128]{1,0:T(8,128)S(1)} %exchange_row_1.1.pot_red.g_pot.refs_1_, f32[256,128]{1,0:T(8,128)S(1)} %get-tuple-element.12.pot_red.pot_keep.refs_1_, s32[552]{0:T(1024)S(1)} %get-tuple-element.14.table), custom_call_target="tpu_custom_call" | custom-call | tf_op jit(solution)/shard_map/row_pass/pallas_call | solution.py:255
  110.1 31.6 %exchange_col_2.1.f_pot = f32[256,128]{1,0:T(8,128)S(1)} custom-call(f32[256,128]{1,0:T(8,128)S(1)} %row_pass.1.refs_0_, f32[256,128]{1,0:T(8,128)S(1)} %get-tuple-element.12.pot_red.pot_keep.refs_1_, f32[256,128]{1,0:T(8,128)S(1)} %bitcast.8), custom_call_target="tpu_custom_call" | custom-call | tf_op jit(solution)/shard_map/exchange_col_2/pallas_call | solution.py:365
  141.7 3.7 %last_pass.1 = (f32[128,128]{1,0:T(8,128)S(1)}, f32[256,128]{1,0:T(8,128)}) custom-call(bf16[64,49152]{1,0:T(8,128)(2,1)S(1)} %get-tuple-element.10.refs_2_.points, f32[256,128]{1,0:T(8,128)S(1)} %exchange_col_2.1.f_pot, f32[128,128]{1,0:T(8,128)S(1)} %exchange_row_1.1.pot_red.g_pot.refs_1_, f32[256,128]{1,0:T(8,128)S(1)} %get-tuple-element.15.half_src, ...), custom_call_target="tpu_custom_call" | custom-call | tf_op jit(solution)/shard_map/last_pass/pallas_call | solution.py:264
  145.4 11.3 %exchange_row_3.1 = f32[128,128]{1,0:T(8,128)S(1)} custom-call(f32[128,128]{1,0:T(8,128)S(1)} %get-tuple-element.17.refs_0_, f32[128,128]{1,0:T(8,128)S(1)} %exchange_row_1.1.pot_red.g_pot.refs_1_, f32[128,128]{1,0:T(8,128)S(1)} %bitcast.10), custom_call_target="tpu_custom_call" | custom-call | tf_op jit(solution)/shard_map/exchange_row_3/pallas_call | solution.py:365
  156.7 0.6 add_bitcast_fusion
  (1 shorter events, 0.0 us)
Async XLA Ops:
  0.6 33.6 %copy-start = (f32[32768]{0:T(1024)S(1)}, f32[32768]{0:T(1024)}, u32[]{:S(2)}) copy-start(f32[32768]{0:T(1024)} %param.8) | copy-start | bytes 393220
  48.0 30.5 %copy-start.1 = (f32[16384]{0:T(1024)S(1)}, f32[16384]{0:T(1024)}, u32[]{:S(2)}) copy-start(f32[16384]{0:T(1024)} %param.9) | copy-start | bytes 196612

commit v2 on v1

--- a/solution.py
+++ b/solution.py
@@ -13,10 +13,13 @@
 EPS = 0.05
 LOG2_SCALE = 20.0 * 1.4426950408889634
 NEG = -1e30
-BIG_GROUP = 32
+BIG_GROUP = 48
+FIRST_GROUP = 24
 SMALL_GROUP = 8
 PAD = 16
 CHUNKS = 4
+SOURCE_CHUNKS = 8
+ROW_SHIFT = 16
 THRESHOLD = 2.0**-90
 CEILING = 2.0**120
 FIRST_BIAS = 40.0
@@ -26,26 +29,19 @@
 MIB = 1024 * 1024
 
 
-def build_pairs(cols_ref, count_ref, table, row_blocks, slots):
-    row_at, col_at = table_starts(table)
-
-    def add(b, n):
-        used = count_ref[0, b]
-        for s in range(slots):
-            table[row_at + n] = b
-            table[col_at + n] = cols_ref[s, b]
-            n = n + (s < used).astype(jnp.int32)
-        return n
-
-    total = lax.fori_loop(0, row_blocks, add, jnp.int32(0), unroll=8)
+TABLE_START = 8
+
+
+def add_pairs(cols_ref, count_ref, table, b, n, slots):
+    for s in range(slots):
+        table[TABLE_START + n + s] = (b << ROW_SHIFT) + cols_ref[s, b]
+    return n + count_ref[0, b]
+
+
+def close_table(table, total):
     for k in range(PAD):
-        table[row_at + total + k] = jnp.int32(-1)
-        table[col_at + total + k] = jnp.int32(-1)
+        table[TABLE_START + total + k] = jnp.int32(-1)
     table[0] = total
-
-
-def table_starts(table):
-    return 8, 8 + (table.shape[0] - 8) // 2
 
 
 def split3(v):
@@ -55,24 +51,27 @@
     return hi, mid, rest - mid
 
 
-def half_norms(points, first, out_ref, start, stop):
+def half_norm(points, first, out_ref, b):
+    blk = points[:, pl.ds(pl.multiple_of((first + b) * BLOCK, BLOCK), BLOCK)].astype(jnp.float32)
+    norm = 0.5 * jnp.sum(blk * blk, 0, keepdims=True)
+    out_ref[pl.ds(2 * b, 1), :] = norm[:, :LANES]
+    out_ref[pl.ds(2 * b + 1, 1), :] = norm[:, LANES:]
+
+
+def half_norms(points, first, out_ref, blocks):
     def one(b, carry):
-        blk = points[:, pl.ds(pl.multiple_of((first + b) * BLOCK, BLOCK), BLOCK)].astype(jnp.float32)
-        norm = 0.5 * jnp.sum(blk * blk, 0, keepdims=True)
-        out_ref[pl.ds(2 * b, 1), :] = norm[:, :LANES]
-        out_ref[pl.ds(2 * b + 1, 1), :] = norm[:, LANES:]
+        half_norm(points, first, out_ref, b)
         return carry
 
-    lax.fori_loop(start, stop, one, 0, unroll=4)
+    lax.fori_loop(0, blocks, one, 0, unroll=4)
 
 
 def lse_pass(
     bias, by_row, points, pot_red, pot_keep, table,
-    rel_ref, red_parts, keep_parts, acc, top, touched,
+    rel_ref, red_parts, keep_parts, acc, top, touched, big=BIG_GROUP, arrive=None,
 ):
     nkeep = rel_ref.shape[0] // 2
     npairs = table[0]
-    keep_at, red_at = table_starts(table) if by_row else table_starts(table)[::-1]
     nred = pot_red.shape[0] // 2
     red_first, keep_first = (nkeep, 0) if by_row else (0, nred)
     shift = bias / LOG2_SCALE
@@ -96,11 +95,11 @@
         return jnp.concatenate(halves, 1)
 
     def scores(p):
-        slot_r = table[red_at + p]
-        slot_k = table[keep_at + p]
-        r = jnp.maximum(slot_r, 0)
-        k = jnp.maximum(slot_k, 0)
-        into = jnp.where(slot_k < 0, nkeep, slot_k)
+        word = table[TABLE_START + p]
+        pair = jnp.maximum(word, 0)
+        row, col = pair >> ROW_SHIFT, pair & ((1 << ROW_SHIFT) - 1)
+        k, r = (row, col) if by_row else (col, row)
+        into = jnp.where(word < 0, nkeep, k)
         rblk = points[:, pl.ds(pl.multiple_of((red_first + r) * BLOCK, BLOCK), BLOCK)]
         kblk = points[:, pl.ds(pl.multiple_of((keep_first + k) * BLOCK, BLOCK), BLOCK)]
         lhs = jnp.concatenate([rblk, rows(red_parts, r, 0, 3)], 0)
@@ -117,18 +116,24 @@
         acc[pl.ds(2 * into + 1, 1), :] += part[:, LANES:]
         touched[pl.ds(2 * into, 2), :] = jnp.ones((2, LANES), jnp.float32)
 
-    def groups(size, base, trips):
-        def group(t, carry):
+    def groups(size, base, trips, here):
+        def group(t, here):
+            first = base + t * size
+            if arrive is not None:
+                last = table[TABLE_START + jnp.minimum(first + size, npairs) - 1]
+                here = arrive(here, last >> ROW_SHIFT)
             for u in range(size):
-                add_pair(base + t * size + u, False)
-            return carry
-
-        lax.fori_loop(0, trips, group, 0)
-
-    whole = (npairs + PAD - 1) // BIG_GROUP
-    left = jnp.maximum(npairs - whole * BIG_GROUP, 0)
-    groups(BIG_GROUP, 0, whole)
-    groups(SMALL_GROUP, whole * BIG_GROUP, (left + SMALL_GROUP - 1) // SMALL_GROUP)
+                add_pair(first + u, False)
+            return here
+
+        return lax.fori_loop(0, trips, group, here)
+
+    whole = (npairs + PAD - 1) // big
+    left = jnp.maximum(npairs - whole * big, 0)
+    here = groups(big, 0, whole, jnp.int32(0))
+    here = groups(SMALL_GROUP, whole * big, (left + SMALL_GROUP - 1) // SMALL_GROUP, here)
+    if arrive is not None:
+        arrive(here, None)
     total = acc[: 2 * nkeep]
     live = touched[: 2 * nkeep] > 0.0
     rel_ref[...] = jnp.where(live, jnp.log2(total) - bias, NEG)
@@ -167,29 +172,54 @@
     row_blocks = rel.shape[0] // 2
     col_blocks = half_tgt.shape[0] // 2
 
-    def chunk(whole, first, sem, c):
-        width = whole.shape[1] // CHUNKS
-        into = pl.ds(first * BLOCK + c * width, width)
-        return pltpu.make_async_copy(whole.at[:, pl.ds(c * width, width)], points.at[:, into], sem.at[c])
+    def chunk(whole, first, sem, chunks, c):
+        width = whole.shape[1] // chunks
+        start = c * width if isinstance(c, int) else pl.multiple_of(c * width, LANES)
+        into = pl.ds(first * BLOCK + start, width)
+        return pltpu.make_async_copy(whole.at[:, pl.ds(start, width)], points.at[:, into], sem.at[c])
 
     list_copies = [
         pltpu.make_async_copy(cols, cols_here, sem_list.at[0]),
         pltpu.make_async_copy(counts, counts_here, sem_list.at[1]),
     ]
-    tgt_copies = [chunk(targets, row_blocks, sem_tgt, c) for c in range(CHUNKS)]
-    src_copies = [chunk(sources, 0, sem_src, c) for c in range(CHUNKS)]
-    for copy in list_copies + tgt_copies + src_copies:
+    tgt_copies = [chunk(targets, row_blocks, sem_tgt, CHUNKS, c) for c in range(CHUNKS)]
+    src_copies = [chunk(sources, 0, sem_src, SOURCE_CHUNKS, c) for c in range(SOURCE_CHUNKS)]
+    ahead = SOURCE_CHUNKS // CHUNKS
+    for copy in list_copies + tgt_copies + src_copies[:ahead]:
         copy.start()
     for copy in list_copies:
         copy.wait()
-    build_pairs(cols_here, counts_here, table, row_blocks, slots)
+
+    parts = col_blocks // 4
+    per_part = row_blocks // parts
+
+    def prepare(t, n):
+        for u in range(4):
+            half_norm(points, row_blocks, half_tgt, 4 * t + u)
+        for u in range(per_part):
+            n = add_pairs(cols_here, counts_here, table, per_part * t + u, n, slots)
+        return n
+
+    total = jnp.int32(0)
     for c, copy in enumerate(tgt_copies):
         copy.wait()
-        half_norms(points, row_blocks, half_tgt, c * col_blocks // CHUNKS, (c + 1) * col_blocks // CHUNKS)
+        for later in src_copies[(c + 1) * ahead : (c + 2) * ahead]:
+            later.start()
+        total = lax.fori_loop(c * parts // CHUNKS, (c + 1) * parts // CHUNKS, prepare, total)
+    close_table(table, total)
     pot_tgt[...] = -half_tgt[...]
-    for copy in src_copies:
-        copy.wait()
-    lse_pass(FIRST_BIAS, True, points, pot_tgt, None, table, rel, *scratch)
+
+    def arrive(here, row):
+        stop = SOURCE_CHUNKS if row is None else row // (row_blocks // SOURCE_CHUNKS) + 1
+
+        def one(c, carry):
+            chunk(sources, 0, sem_src, SOURCE_CHUNKS, c).wait()
+            return carry
+
+        lax.fori_loop(here, stop, one, 0)
+        return jnp.maximum(here, stop)
+
+    lse_pass(FIRST_BIAS, True, points, pot_tgt, None, table, rel, *scratch, big=FIRST_GROUP, arrive=arrive)
 
 
 def last_kernel(bias, points, f_pot, g_pot, half_src, table, rel, f_final, f_here, sem, *scratch):
@@ -230,7 +260,7 @@
             potential(nkeep),
             jax.ShapeDtypeStruct((sources.shape[0], sources.shape[1] + targets.shape[1]), sources.dtype),
             potential(nred),
-            jax.ShapeDtypeStruct((8 + 2 * (nkeep * slots + PAD),), jnp.int32),
+            jax.ShapeDtypeStruct((TABLE_START + nkeep * slots + PAD,), jnp.int32),
         ),
         in_specs=[HBM, HBM, HBM, HBM],
         out_specs=(VMEM, VMEM, VMEM, SMEM),
@@ -238,7 +268,7 @@
             pltpu.VMEM((2 * nred, LANES), jnp.float32),
             pltpu.SMEM(cols.shape, jnp.int32),
             pltpu.SMEM(counts.shape, jnp.int32),
-            pltpu.SemaphoreType.DMA((CHUNKS,)),
+            pltpu.SemaphoreType.DMA((SOURCE_CHUNKS,)),
             pltpu.SemaphoreType.DMA((CHUNKS,)),
             pltpu.SemaphoreType.DMA((2,)),
         ]
@@ -333,7 +363,7 @@
     for copy in first:
         copy.start()
     if with_norms:
-        half_norms(points, 0, norms, 0, rel.shape[0] // 2)
+        half_norms(points, 0, norms, rel.shape[0] // 2)
     own = rel[mine]
     fetch.wait()
     base = EPS * weights[...]

time: 157 us -> 172 us (1.096)
  Pallas kernels: 156 us -> 170 us
    pallas_call x4, Pallas kernels: 84.6 us -> 105 us  [exchange(): pl.pallas_call(functools.partial(exchange_kernel, axis, sides, has_old, w...]
    pallas_call x2, Pallas kernels: 34.2 us -> 31.2 us  [later_pass(): pl.pallas_call(functools.partial(lse_pass, bias, by_row), out_shape=poten...]
    pallas_call x1, Pallas kernels: 33.5 us -> 30.8 us  [first_pass(): pl.pallas_call(functools.partial(first_kernel, slots), out_shape=(potenti...]
where the time goes in v2:
time: 172 us
  Pallas kernels  170 us (99%)
    pallas_call x4, Pallas kernels, exchange(): pl.pallas_call(functools.partial(exchange_kernel, axis, sides, has_old, w...  105 us
    pallas_call x2, Pallas kernels, later_pass(): pl.pallas_call(functools.partial(lse_pass, bias, by_row), out_shape=poten...  31.2 us
    pallas_call x1, Pallas kernels, first_pass(): pl.pallas_call(functools.partial(first_kernel, slots), out_shape=(potenti...  30.8 us
    pallas_call x1, Pallas kernels, later_pass(): pl.pallas_call(functools.partial(last_kernel, bias), out_shape=(potential...  3.53 us

profile of v2, /device:TPU:1, one launch (start us, length us, event | category | flops | bytes accessed | tf_op | source)
XLA Modules:
  0.0 171.5 jit_solution(11484765448348342350)
XLA Ops:
  0.6 0.0 copy-start
  0.6 30.8 %first_pass.1 = (f32[256,128]{1,0:T(8,128)S(1)}, bf16[64,49152]{1,0:T(8,128)(2,1)S(1)}, f32[128,128]{1,0:T(8,128)S(1)}, s32[280]{0:T(512)S(1)}) custom-call(bf16[64,32768]{1,0:T(8,128)(2,1)} %sources.1, bf16[64,16384]{1,0:T(8,128)(2,1)} %targets.1, s32[2,128]{1,0:T(2,128)} %bitcast.11, s32[1,128]{1,0:T(1,128)} %bitcast.12), custom_call_target="tpu_custom_call" | custom-call | tf_op jit(solution)/shard_map/first_pass/pallas_call | solution.py:257
  31.5 0.0 copy-done
  31.5 45.3 %exchange_col_0.1 = (f32[256,128]{1,0:T(8,128)S(1)}, f32[256,128]{1,0:T(8,128)S(1)}) custom-call(f32[256,128]{1,0:T(8,128)S(1)} %get-tuple-element.11.refs_0_, f32[256,128]{1,0:T(8,128)S(1)} %bitcast.7, bf16[64,49152]{1,0:T(8,128)(2,1)S(1)} %get-tuple-element.10.refs_2_.points), custom_call_target="tpu_custom_call" | custom-call | tf_op jit(solution)/shard_map/exchange_col_0/pallas_call | solution.py:395
  76.8 0.0 copy-start.1
  76.8 27.8 %col_pass.1.refs_0_ = f32[128,128]{1,0:T(8,128)S(1)} custom-call(bf16[64,49152]{1,0:T(8,128)(2,1)S(1)} %get-tuple-element.10.refs_2_.points, f32[256,128]{1,0:T(8,128)S(1)} %get-tuple-element.12.pot_red.pot_keep.refs_1_, f32[128,128]{1,0:T(8,128)S(1)} %neg.3.pot_keep.refs_1_, s32[280]{0:T(512)S(1)} %get-tuple-element.14.table), custom_call_target="tpu_custom_call" | custom-call | tf_op jit(solution)/shard_map/col_pass/pallas_call | solution.py:285
  104.6 0.0 copy-done.1
  104.6 8.2 %exchange_row_1.1.pot_red.g_pot.refs_1_ = f32[128,128]{1,0:T(8,128)S(1)} custom-call(f32[128,128]{1,0:T(8,128)S(1)} %col_pass.1.refs_0_, f32[128,128]{1,0:T(8,128)S(1)} %neg.3.pot_keep.refs_1_, f32[128,128]{1,0:T(8,128)S(1)} %bitcast.9), custom_call_target="tpu_custom_call" | custom-call | tf_op jit(solution)/shard_map/exchange_row_1/pallas_call | solution.py:395
  112.8 3.4 %row_pass.1.refs_0_ = f32[256,128]{1,0:T(8,128)S(1)} custom-call(bf16[64,49152]{1,0:T(8,128)(2,1)S(1)} %get-tuple-element.10.refs_2_.points, f32[128,128]{1,0:T(8,128)S(1)} %exchange_row_1.1.pot_red.g_pot.refs_1_, f32[256,128]{1,0:T(8,128)S(1)} %get-tuple-element.12.pot_red.pot_keep.refs_1_, s32[280]{0:T(512)S(1)} %get-tuple-element.14.table), custom_call_target="tpu_custom_call" | custom-call | tf_op jit(solution)/shard_map/row_pass/pallas_call | solution.py:285
  116.2 42.8 %exchange_col_2.1.f_pot = f32[256,128]{1,0:T(8,128)S(1)} custom-call(f32[256,128]{1,0:T(8,128)S(1)} %row_pass.1.refs_0_, f32[256,128]{1,0:T(8,128)S(1)} %get-tuple-element.12.pot_red.pot_keep.refs_1_, f32[256,128]{1,0:T(8,128)S(1)} %bitcast.8), custom_call_target="tpu_custom_call" | custom-call | tf_op jit(solution)/shard_map/exchange_col_2/pallas_call | solution.py:395
  159.0 3.5 %last_pass.1 = (f32[128,128]{1,0:T(8,128)S(1)}, f32[256,128]{1,0:T(8,128)}) custom-call(bf16[64,49152]{1,0:T(8,128)(2,1)S(1)} %get-tuple-element.10.refs_2_.points, f32[256,128]{1,0:T(8,128)S(1)} %exchange_col_2.1.f_pot, f32[128,128]{1,0:T(8,128)S(1)} %exchange_row_1.1.pot_red.g_pot.refs_1_, f32[256,128]{1,0:T(8,128)S(1)} %get-tuple-element.15.half_src, ...), custom_call_target="tpu_custom_call" | custom-call | tf_op jit(solution)/shard_map/last_pass/pallas_call | solution.py:294
  162.6 8.3 %exchange_row_3.1 = f32[128,128]{1,0:T(8,128)S(1)} custom-call(f32[128,128]{1,0:T(8,128)S(1)} %get-tuple-element.17.refs_0_, f32[128,128]{1,0:T(8,128)S(1)} %exchange_row_1.1.pot_red.g_pot.refs_1_, f32[128,128]{1,0:T(8,128)S(1)} %bitcast.10), custom_call_target="tpu_custom_call" | custom-call | tf_op jit(solution)/shard_map/exchange_row_3/pallas_call | solution.py:395
  170.9 0.6 add_bitcast_fusion
  (1 shorter events, 0.0 us)
Async XLA Ops:
  0.6 30.8 %copy-start = (f32[32768]{0:T(1024)S(1)}, f32[32768]{0:T(1024)}, u32[]{:S(2)}) copy-start(f32[32768]{0:T(1024)} %param.8) | copy-start | bytes 393220
  76.8 27.8 %copy-start.1 = (f32[16384]{0:T(1024)S(1)}, f32[16384]{0:T(1024)}, u32[]{:S(2)}) copy-start(f32[16384]{0:T(1024)} %param.9) | copy-start | bytes 196612
